TPU v7x, 512 devices: a whole 4x8x8 slice. The times are simulated.
512 devices in a mesh: dp: 32 (over x, z), table: 16 (over y, core).
Axes of the slice: x: 4, y: 8, z: 8, core: 2. Of those that a mesh axis runs over, the one named last changes fastest.
Arguments:
- dense_feats: bfloat16 [65536, 13], P(('dp', 'table')), may hold values from -6 to 6
- lookup_ids: int32 [32, 8, 65536], P('table', None, 'dp'), may hold values from 0 to 2047
- lookup_counts: int32 [32, 65536], P('table', 'dp'), may hold values from 0 to 8
- shard_table: int32 [32], replicated, may hold values from 0 to 25, as said below
- embed_tables: bfloat16 [32, 2048, 128], P('table'), may hold values from -6 to 6
- first_layer: bfloat16 [13, 512], replicated, may hold values from -1.75 to 1.75
- first_offset: float32 [512], replicated, may hold values from -3 to 3
- second_layer: bfloat16 [512, 256], replicated, may hold values from -0.25 to 0.25
- second_offset: float32 [256], replicated, may hold values from -3 to 3
- third_layer: bfloat16 [256, 128], replicated, may hold values from -0.375 to 0.375
- third_offset: float32 [128], replicated, may hold values from -3 to 3
- cross_down: bfloat16 [3456, 512], P(None, 'table'), may hold values from -0.109375 to 0.109375
- cross_up: bfloat16 [512, 3456], P('table'), may hold values from -0.25 to 0.25
- cross_bias: float32 [3456], replicated, may hold values from -3 to 3
- cotangent: bfloat16 [65536, 3456], P(('dp', 'table')), may hold values from -0.059814453 to 0.059814453
Outputs:
- table_grad: float32 [32, 2048, 128], P('table', 'dp')
- first_layer_grad: float32 [13, 512], replicated
- first_offset_grad: float32 [512], replicated
- second_layer_grad: float32 [512, 256], replicated
- second_offset_grad: float32 [256], replicated
- third_layer_grad: float32 [256, 128], replicated
- third_offset_grad: float32 [128], replicated
- cross_bias_grad: float32 [3456], replicated
Inputs may be any that keep to these rules, and one draw needn't show every extreme that they name: `shard_table`: every table has at least one shard.
All inputs are finite; a program needn't handle non-finite values.
Results may differ from a plain program's by a relative error of at most 0.0085.
Values may be sent and summed in bfloat16 or wider, within the bound.
No kernel may reach another device: no remote copies, remote signals or barrier semaphores. Data moves between devices by JAX's collectives and lax.ppermute only.
A program may use at most 64 MiB of HBM per device.

v0:
```python
import math
import jax
import jax.numpy as jnp
from jax import lax
from jax.sharding import PartitionSpec as P

TABLES = 26


def silu_slope(value):
    sigmoid = 1.0 / (1.0 + jnp.exp(-value))
    return sigmoid * (1.0 + value * (1.0 - sigmoid))


def hit_counts(index_block, count_block, row_total):
    iota_rows = lax.broadcasted_iota(jnp.int32, (index_block.shape[1], row_total), 1)
    totals = jnp.zeros((index_block.shape[1], row_total), jnp.bfloat16)
    for slot_index in range(index_block.shape[0]):
        matched = (index_block[slot_index][:, None] == iota_rows) & (
            count_block[:, None] > slot_index
        )
        totals = totals + matched.astype(jnp.bfloat16)
    return totals


def split_blocks(shard_index, shard_count, block_size):
    hot_total, batch_total = shard_index.shape
    blocks = batch_total // block_size
    index_blocks = shard_index.reshape(hot_total, blocks, block_size).transpose(1, 0, 2)
    count_blocks = shard_count.reshape(blocks, block_size)
    return (index_blocks, count_blocks, blocks)


def pool_shard(table_rows, shard_index, shard_count, block_size):
    index_blocks, count_blocks, blocks = split_blocks(shard_index, shard_count, block_size)

    def pool_one_block(inputs):
        hit_table = hit_counts(inputs[0], inputs[1], table_rows.shape[0])
        return jnp.dot(hit_table, table_rows, preferred_element_type=jnp.float32)

    pooled = lax.map(pool_one_block, (index_blocks, count_blocks))
    return pooled.reshape(shard_index.shape[1], table_rows.shape[1])


def shard_gradient(shard_index, shard_count, grad_rows, row_total, block_size):
    index_blocks, count_blocks, blocks = split_blocks(shard_index, shard_count, block_size)
    grad_blocks = grad_rows.reshape(blocks, block_size, grad_rows.shape[1])

    def shard_one_block(running, inputs):
        hit_table = hit_counts(inputs[0], inputs[1], row_total)
        update = lax.dot_general(
            hit_table, inputs[2], (((0,), (0,)), ((), ())), preferred_element_type=jnp.float32
        )
        return (running + update, None)

    result, unused = lax.scan(
        shard_one_block,
        jnp.zeros((row_total, grad_rows.shape[1]), jnp.float32),
        (index_blocks, count_blocks, grad_blocks),
    )
    return result


def bottom_pass(
    dense_rows, first_layer, first_offset, second_layer, second_offset, third_layer, third_offset
):
    first_pre = jnp.dot(dense_rows, first_layer, preferred_element_type=jnp.float32) + first_offset
    first_act = jax.nn.silu(first_pre).astype(jnp.bfloat16)
    second_pre = (
        jnp.dot(first_act, second_layer, preferred_element_type=jnp.float32) + second_offset
    )
    second_act = jax.nn.silu(second_pre).astype(jnp.bfloat16)
    third_pre = jnp.dot(second_act, third_layer, preferred_element_type=jnp.float32) + third_offset
    bottom_out = jax.nn.silu(third_pre).astype(jnp.bfloat16)
    return (bottom_out, (first_pre, first_act, second_pre, second_act, third_pre))


def bottom_back(dense_rows, saved, second_layer, third_layer, bottom_grad):
    first_pre, first_act, second_pre, second_act, third_pre = saved
    contract = (((0,), (0,)), ((), ()))
    back_dims = (((1,), (1,)), ((), ()))
    third_delta = (silu_slope(third_pre) * bottom_grad.astype(jnp.float32)).astype(jnp.bfloat16)
    third_grad = lax.dot_general(
        second_act, third_delta, contract, preferred_element_type=jnp.float32
    )
    third_bias = jnp.sum(third_delta.astype(jnp.float32), axis=0)
    second_back = lax.dot_general(
        third_delta, third_layer, back_dims, preferred_element_type=jnp.float32
    )
    second_delta = (silu_slope(second_pre) * second_back).astype(jnp.bfloat16)
    second_grad = lax.dot_general(
        first_act, second_delta, contract, preferred_element_type=jnp.float32
    )
    second_bias = jnp.sum(second_delta.astype(jnp.float32), axis=0)
    first_back = lax.dot_general(
        second_delta, second_layer, back_dims, preferred_element_type=jnp.float32
    )
    first_delta = (silu_slope(first_pre) * first_back).astype(jnp.bfloat16)
    first_grad = lax.dot_general(
        dense_rows, first_delta, contract, preferred_element_type=jnp.float32
    )
    first_bias = jnp.sum(first_delta.astype(jnp.float32), axis=0)
    return (first_grad, first_bias, second_grad, second_bias, third_grad, third_bias)


def local(
    dense_feats,
    lookup_ids,
    lookup_counts,
    shard_table,
    embed_tables,
    first_layer,
    first_offset,
    second_layer,
    second_offset,
    third_layer,
    third_offset,
    cross_down,
    cross_up,
    cross_bias,
    cotangent,
):
    local_shards, row_total, width = embed_tables.shape
    batch_group = lookup_ids.shape[2]
    block_size = math.gcd(batch_group, 1024)
    examples = dense_feats.shape[0]
    back_dims = (((1,), (1,)), ((), ()))
    pooled = jnp.stack(
        [
            pool_shard(
                embed_tables[shard_pos], lookup_ids[shard_pos], lookup_counts[shard_pos], block_size
            )
            for shard_pos in range(local_shards)
        ],
        axis=1,
    ).astype(jnp.bfloat16)
    arrived = lax.all_to_all(pooled, "table", split_axis=0, concat_axis=1, tiled=True)
    table_onehot = (
        shard_table[:, None] == lax.broadcasted_iota(jnp.int32, (shard_table.shape[0], TABLES), 1)
    ).astype(jnp.bfloat16)
    table_pooled = jnp.einsum(
        "bse,st->bte", arrived, table_onehot, preferred_element_type=jnp.float32
    ).astype(jnp.bfloat16)
    bottom_out, saved = bottom_pass(
        dense_feats,
        first_layer,
        first_offset,
        second_layer,
        second_offset,
        third_layer,
        third_offset,
    )
    cross_input = jnp.concatenate([bottom_out[:, None, :], table_pooled], axis=1).reshape(
        examples, -1
    )
    down_whole = lax.all_gather(cross_down, "table", axis=1, tiled=True)
    up_whole = lax.all_gather(cross_up, "table", axis=0, tiled=True)
    low_rank = jnp.dot(cross_input, down_whole, preferred_element_type=jnp.float32).astype(
        jnp.bfloat16
    )
    mixing = jnp.dot(low_rank, up_whole, preferred_element_type=jnp.float32) + cross_bias
    cot_float = cotangent.astype(jnp.float32)
    mix_grad = cot_float * cross_input.astype(jnp.float32)
    bias_part = jnp.sum(mix_grad, axis=0)
    rank_grad = lax.dot_general(
        mix_grad.astype(jnp.bfloat16), up_whole, back_dims, preferred_element_type=jnp.float32
    ).astype(jnp.bfloat16)
    input_grad = (
        cot_float * (mixing + 1.0)
        + lax.dot_general(rank_grad, down_whole, back_dims, preferred_element_type=jnp.float32)
    ).astype(jnp.bfloat16)
    input_grad = input_grad.reshape(examples, TABLES + 1, width)
    bottom_grad = input_grad[:, 0, :]
    shard_grads = jnp.einsum(
        "bte,st->bse", input_grad[:, 1:, :], table_onehot, preferred_element_type=jnp.float32
    ).astype(jnp.bfloat16)
    returned = lax.all_to_all(shard_grads, "table", split_axis=1, concat_axis=0, tiled=True)
    local_grad = jnp.stack(
        [
            shard_gradient(
                lookup_ids[shard_pos],
                lookup_counts[shard_pos],
                returned[:, shard_pos, :],
                row_total,
                block_size,
            )
            for shard_pos in range(local_shards)
        ],
        axis=0,
    )
    table_grad = lax.psum_scatter(local_grad, "dp", scatter_dimension=1, tiled=True)
    partial_grads = bottom_back(dense_feats, saved, second_layer, third_layer, bottom_grad)
    summed = lax.psum(
        (
            partial_grads[0],
            partial_grads[1],
            partial_grads[2],
            partial_grads[3],
            partial_grads[4],
            partial_grads[5],
            bias_part,
        ),
        ("dp", "table"),
    )
    return (table_grad, summed[0], summed[1], summed[2], summed[3], summed[4], summed[5], summed[6])


def solution(mesh):
    placed = (
        P(("dp", "table"), None),
        P("table", None, "dp"),
        P("table", "dp"),
        P(),
        P("table", None, None),
        P(),
        P(),
        P(),
        P(),
        P(),
        P(),
        P(None, "table"),
        P("table", None),
        P(),
        P(("dp", "table"), None),
    )
    return jax.shard_map(
        local,
        mesh=mesh,
        in_specs=placed,
        out_specs=(P("table", "dp", None), P(), P(), P(), P(), P(), P(), P()),
        check_vma=False,
    )
```

profile of v0, /device:TPU:8, one launch (start us, length us, event | category | flops | bytes accessed | tf_op | source)
XLA Modules:
  0.0 667.9 jit_solution(7342675556975713716)
XLA Ops:
  10.4 1.3 slice_bitcast_fusion.1
  11.8 33.8 %while.42 = (s32[]{:T(128)}, bf16[2,1024,128]{2,1,0:T(8,128)(2,1)S(1)}, s32[2,8,1024]{2,1,0:T(8,128)S(1)}, s32[2,1024]{1,0:T(2,128)S(1)}, bf16[2048,128]{1,0:T(8...) while((s32[]{:T(128)}, ...), condition=%wide.region_1.2_spmd, body=%wide.region_0.1_spmd.sunk | while | flops 620765184 | bytes 1167617 | solution.py:41
  11.9 16.7 %fusion.244 = bf16[2,1024,128]{2,1,0:T(8,128)(2,1)S(1)} fusion(bf16[2,1024,128]{2,1,0:T(8,128)(2,1)S(1)} %get-tuple-element.590, s32[]{:T(128)} %get-tuple-element.589, bf16[2048,128]{1,0:T(8,128)(2,1)S(1)} %get-tuple-element.607, s32[1024]{0:T(1024)S(1)} %bitcast.227, s32[1024]{0:T(1024)S(1)} %bitcast.221, s32[1024]{0:T(1024)S(1)} %bitcast.222, ...), kind=kOutput, calls=%fused_computation.41.clone.1 | convolution fusion | flops 620756992 | bytes 1089540 | tf_op jit(solution)/shard_map/while/body/eval_jaxpr/dot_general | solution.py:39
  28.8 16.7 %fusion.244 = bf16[2,1024,128]{2,1,0:T(8,128)(2,1)S(1)} fusion(bf16[2,1024,128]{2,1,0:T(8,128)(2,1)S(1)} %get-tuple-element.590, s32[]{:T(128)} %get-tuple-element.589, bf16[2048,128]{1,0:T(8,128)(2,1)S(1)} %get-tuple-element.607, s32[1024]{0:T(1024)S(1)} %bitcast.227, s32[1024]{0:T(1024)S(1)} %bitcast.221, s32[1024]{0:T(1024)S(1)} %bitcast.222, ...), kind=kOutput, calls=%fused_computation.41.clone.1 | convolution fusion | flops 620756992 | bytes 1089540 | tf_op jit(solution)/shard_map/while/body/eval_jaxpr/dot_general | solution.py:39
  45.7 33.8 %while.43 = (s32[]{:T(128)}, bf16[2,1024,128]{2,1,0:T(8,128)(2,1)S(1)}, s32[2,8,1024]{2,1,0:T(8,128)S(1)}, s32[2,1024]{1,0:T(2,128)S(1)}, bf16[2048,128]{1,0:T(8...) while((s32[]{:T(128)}, ...), condition=%wide.region_3.4_spmd, body=%wide.region_2.3_spmd.sunk | while | flops 620765184 | bytes 1167617 | solution.py:41
  45.8 16.7 %fusion.247 = bf16[2,1024,128]{2,1,0:T(8,128)(2,1)S(1)} fusion(bf16[2,1024,128]{2,1,0:T(8,128)(2,1)S(1)} %get-tuple-element.548, s32[]{:T(128)} %get-tuple-element.547, bf16[2048,128]{1,0:T(8,128)(2,1)S(1)} %get-tuple-element.565, s32[1024]{0:T(1024)S(1)} %bitcast.235, s32[1024]{0:T(1024)S(1)} %bitcast.229, s32[1024]{0:T(1024)S(1)} %bitcast.230, ...), kind=kOutput, calls=%fused_computation.100.clone.1 | convolution fusion | flops 620756992 | bytes 1089540 | tf_op jit(solution)/shard_map/while/body/eval_jaxpr/dot_general | solution.py:39
  62.7 16.7 %fusion.247 = bf16[2,1024,128]{2,1,0:T(8,128)(2,1)S(1)} fusion(bf16[2,1024,128]{2,1,0:T(8,128)(2,1)S(1)} %get-tuple-element.548, s32[]{:T(128)} %get-tuple-element.547, bf16[2048,128]{1,0:T(8,128)(2,1)S(1)} %get-tuple-element.565, s32[1024]{0:T(1024)S(1)} %bitcast.235, s32[1024]{0:T(1024)S(1)} %bitcast.229, s32[1024]{0:T(1024)S(1)} %bitcast.230, ...), kind=kOutput, calls=%fused_computation.100.clone.1 | convolution fusion | flops 620756992 | bytes 1089540 | tf_op jit(solution)/shard_map/while/body/eval_jaxpr/dot_general | solution.py:39
  79.6 9.5 %copy.44 = bf16[2048,2,128]{2,1,0:T(2,128)(2,1)} copy(bf16[2048,2,128]{2,0,1:T(8,128)(2,1)S(1)} %pad_maximum_fusion.1) | data formatting | bytes 2097152 | tf_op jit(solution)/shard_map/stack | solution.py:128
  89.1 9.8 %all-to-all-start = ((bf16[2048,2,128]{2,1,0:T(2,128)(2,1)}), bf16[2048,2,128]{2,1,0:T(2,128)(2,1)S(1)}, u32[]{:S(2)}, u32[]{:S(2)}) async-start(bf16[2048,2,128]{2,1,0:T(2,128)(2,1)} %copy.44), calls=%async_computation | async-start | bytes 2097152 | tf_op jit(solution)/shard_map/all_to_all | solution.py:137
  99.9 24.2 %all-to-all-done = bf16[2048,2,128]{2,1,0:T(2,128)(2,1)S(1)} async-done(((bf16[2048,2,128]{2,1,0:T(2,128)(2,1)}), bf16[2048,2,128]{2,1,0:T(2,128)(2,1)S(1)}, u32[]{:S(2)}, u32[]{:S(2)}) %all-to-all-start) | async-done | bytes 1048608 | tf_op jit(solution)/shard_map/all_to_all | solution.py:137
  124.2 1.1 copy.46
  126.4 1.3 copy.49
  127.7 1.0 copy.50
  128.8 6.5 fusion.187
  135.3 5.4 fusion.188
  142.7 1.9 copy.52
  145.2 1.4 copy.53
  146.6 6.3 all-to-all-start.1
  155.3 1.1 fusion.205
  156.4 21.2 %all-to-all-done.1 = bf16[128,32,128]{2,0,1:T(8,128)(2,1)S(1)} async-done(((bf16[128,32,128]{2,0,1:T(8,128)(2,1)}), bf16[128,32,128]{2,0,1:T(8,128)(2,1)S(1)}, u32[]{:S(2)}, u32[]{:S(2)}) %all-to-all-start.1) | async-done | bytes 1048608 | tf_op jit(solution)/shard_map/all_to_all | solution.py:177
  177.9 30.7 %while.44 = (s32[]{:T(128)}, f32[2048,128]{1,0:T(8,128)}, s32[2,8,1024]{2,1,0:T(8,128)S(1)}, s32[2,1024]{1,0:T(2,128)S(1)}, bf16[2,1024,128]{2,1,0:T(8,128)(2,1)...) while((s32[]{:T(128)}, f32[2048,128]{1,0:T(8,128)}, ...), condition=%wide.region_5.6_spmd.clone, body=%wide.region_4.5_spmd.clone.sunk | while | flops 621289472 | bytes 2478347 | solution.py:56
  178.2 14.5 %fusion.250 = f32[2048,128]{1,0:T(8,128)} fusion(s32[1024]{0:T(1024)S(1)} %bitcast.211, s32[1024]{0:T(1024)S(1)} %bitcast.205, s32[1024]{0:T(1024)S(1)} %bitcast.206, s32[1024]{0:T(1024)S(1)} %bitcast.207, s32[1024]{0:T(1024)S(1)} %bitcast.208, s32[1024]{0:T(1024)S(1)} %bitcast.209, s32[1024]{0:T(1024)S(1)} %bitcast.210, s32[1024]{0:T(1024)S(1)} %bitcast.204, ...), kind=kOutput, calls=%fused_computation.166.clone.1 | convolution fusion | flops 621281280 | bytes 2400261 | tf_op jit(solution)/shard_map/while/body/eval_jaxpr/dot_general | solution.py:51
  192.9 15.7 %fusion.250 = f32[2048,128]{1,0:T(8,128)} fusion(s32[1024]{0:T(1024)S(1)} %bitcast.211, s32[1024]{0:T(1024)S(1)} %bitcast.205, s32[1024]{0:T(1024)S(1)} %bitcast.206, s32[1024]{0:T(1024)S(1)} %bitcast.207, s32[1024]{0:T(1024)S(1)} %bitcast.208, s32[1024]{0:T(1024)S(1)} %bitcast.209, s32[1024]{0:T(1024)S(1)} %bitcast.210, s32[1024]{0:T(1024)S(1)} %bitcast.204, ...), kind=kOutput, calls=%fused_computation.166.clone.1 | convolution fusion | flops 621281280 | bytes 2400261 | tf_op jit(solution)/shard_map/while/body/eval_jaxpr/dot_general | solution.py:51
  208.6 27.9 %while.45 = (s32[]{:T(128)}, f32[2048,128]{1,0:T(8,128)S(1)}, s32[2,8,1024]{2,1,0:T(8,128)S(1)}, s32[2,1024]{1,0:T(2,128)S(1)}, bf16[2,1024,128]{2,1,0:T(8,128)(...) while((s32[]{:T(128)}, f32[2048,128]{1,0:T(8,128)S(1)}, ...), condition=%wide.region_7.8_spmd.clone, body=%wide.region_6.7_spmd.clone.sunk | while | flops 621289472 | bytes 2478347 | solution.py:56
  209.0 13.7 %fusion.253 = f32[2048,128]{1,0:T(8,128)S(1)} fusion(s32[1024]{0:T(1024)S(1)} %bitcast.219, s32[1024]{0:T(1024)S(1)} %bitcast.213, s32[1024]{0:T(1024)S(1)} %bitcast.214, s32[1024]{0:T(1024)S(1)} %bitcast.215, s32[1024]{0:T(1024)S(1)} %bitcast.216, s32[1024]{0:T(1024)S(1)} %bitcast.217, s32[1024]{0:T(1024)S(1)} %bitcast.218, ...), kind=kOutput, calls=%fused_computation.235.clone.1 | convolution fusion | flops 621281280 | bytes 2400261 | tf_op jit(solution)/shard_map/while/body/eval_jaxpr/dot_general | solution.py:51
  222.8 13.7 %fusion.253 = f32[2048,128]{1,0:T(8,128)S(1)} fusion(s32[1024]{0:T(1024)S(1)} %bitcast.219, s32[1024]{0:T(1024)S(1)} %bitcast.213, s32[1024]{0:T(1024)S(1)} %bitcast.214, s32[1024]{0:T(1024)S(1)} %bitcast.215, s32[1024]{0:T(1024)S(1)} %bitcast.216, s32[1024]{0:T(1024)S(1)} %bitcast.217, s32[1024]{0:T(1024)S(1)} %bitcast.218, ...), kind=kOutput, calls=%fused_computation.235.clone.1 | convolution fusion | flops 621281280 | bytes 2400261 | tf_op jit(solution)/shard_map/while/body/eval_jaxpr/dot_general | solution.py:51
  236.5 2.9 pad_maximum_fusion
  240.2 104.6 %all-reduce = (f32[13,512]{1,0:T(8,128)}, f32[512]{0:T(512)}, f32[256]{0:T(256)}, f32[128]{0:T(128)}, f32[3456]{0:T(1024)}) all-reduce(f32[13,512]{1,0:T(8,128)S(1)} %convolution_bitcast_fusion, f32[512]{0:T(512)S(1)} %get-tuple-element.277, f32[256]{0:T(256)S(1)} %copy-done.15, ...), channel_id=1, replica_groups=mesh['dp'=32,'table'=16] {'dp','table'}, use_global_device_ids=true, to_apply=%region_9.10 | all-reduce | flops 11008 | bytes 88064 | tf_op jit(solution)/shard_map/psum | solution.py:193
  344.8 87.7 %all-reduce.4.cloned.1.call-done = (f32[512,256]{1,0:T(8,128)}, f32[256,128]{1,0:T(8,128)}) async-done(((f32[512,256]{1,0:T(8,128)}, f32[256,128]{1,0:T(8,128)}), (f32[512,256]{1,0:T(8,128)}, f32[256,128]{1,0:T(8,128)})) %all-reduce.4.cloned.1.call-update) | async-done | bytes 655376 | tf_op jit(solution)/shard_map/psum | solution.py:193
  432.5 225.0 %reduce-scatter.2.cloned.1.call-done = f32[2,64,128]{2,1,0:T(8,128)} async-done(((f32[2,2048,128]{2,1,0:T(8,128)}), f32[2,64,128]{2,1,0:T(8,128)}) %reduce-scatter.2.cloned.1.call-update) | async-done | bytes 65552 | tf_op jit(solution)/shard_map/reduce_scatter | solution.py:191
  657.5 1.9 copy.85
  659.4 1.6 copy.86
  (102 shorter events, 12.5 us)
Async XLA Ops:
  7.2 92.0 %copy-start = (bf16[512,256]{1,0:T(8,128)(2,1)S(1)}, bf16[512,256]{1,0:T(8,128)(2,1)}, u32[]{:S(2)}) copy-start(bf16[512,256]{1,0:T(8,128)(2,1)} %param.30) | copy-start | bytes 786436
  7.2 121.6 %all-gather.3.cloned.1.call-start = ((), (), s32[]{:S(2)}) async-start(), calls=%async_computation.3 | async-start | bytes 3760128 | tf_op jit(solution)/shard_map/all_gather | solution.py:156
  7.9 120.9 %all-gather.5.cloned.1.call-start = ((), (), s32[]{:S(2)}) async-start(), calls=%async_computation.4 | async-start | bytes 3760128 | tf_op jit(solution)/shard_map/all_gather | solution.py:157
  79.5 19.5 %copy-start.8 = (bf16[13,512]{1,0:T(8,128)(2,1)S(1)}, bf16[13,512]{1,0:T(8,128)(2,1)}, u32[]{:S(2)}) copy-start(bf16[13,512]{1,0:T(8,128)(2,1)} %param.28) | copy-start | bytes 39940
  79.5 19.5 %copy-start.9 = (bf16[128,13]{0,1:T(8,128)(2,1)S(1)}, bf16[128,13]{0,1:T(8,128)(2,1)}, u32[]{:S(2)}) copy-start(bf16[128,13]{0,1:T(8,128)(2,1)} %param.23) | copy-start | bytes 9988
  79.5 19.5 %copy-start.11 = (f32[512]{0:T(512)S(1)}, f32[512]{0:T(512)}, u32[]{:S(2)}) copy-start(f32[512]{0:T(512)} %param.29) | copy-start | bytes 6148
  79.5 19.7 %copy-start.18 = (f32[256]{0:T(256)S(1)}, f32[256]{0:T(256)}, u32[]{:S(2)}) copy-start(f32[256]{0:T(256)} %param.31) | copy-start | bytes 3076
  79.5 19.9 %copy-start.16 = (bf16[256,128]{1,0:T(8,128)(2,1)S(1)}, bf16[256,128]{1,0:T(8,128)(2,1)}, u32[]{:S(2)}) copy-start(bf16[256,128]{1,0:T(8,128)(2,1)} %param.32) | copy-start | bytes 196612
  79.5 19.9 %copy-start.19 = (f32[128]{0:T(128)S(1)}, f32[128]{0:T(128)}, u32[]{:S(2)}) copy-start(f32[128]{0:T(128)} %param.33) | copy-start | bytes 1540
  89.1 34.9 %all-to-all-start = ((bf16[2048,2,128]{2,1,0:T(2,128)(2,1)}), bf16[2048,2,128]{2,1,0:T(2,128)(2,1)S(1)}, u32[]{:S(2)}, u32[]{:S(2)}) async-start(bf16[2048,2,128]{2,1,0:T(2,128)(2,1)} %copy.44), calls=%async_computation | async-start | bytes 2097152 | tf_op jit(solution)/shard_map/all_to_all | solution.py:137
  99.0 26.3 %copy-start.12 = (s32[32]{0:T(128)S(1)}, s32[32]{0:T(128)}, u32[]{:S(2)}) copy-start(s32[32]{0:T(128)} %param.26) | copy-start | bytes 388
  99.2 56.1 %copy-start.6 = (f32[128,512]{1,0:T(8,128)}, f32[128,512]{1,0:T(8,128)S(1)}, u32[]{:S(2)}) copy-start(f32[128,512]{1,0:T(8,128)S(1)} %convolution_add_fusion.2) | copy-start | bytes 786436
  99.5 26.4 %copy-start.20 = (f32[128,256]{1,0:T(8,128)}, f32[128,256]{1,0:T(8,128)S(1)}, u32[]{:S(2)}) copy-start(f32[128,256]{1,0:T(8,128)S(1)} %convolution_add_fusion.3) | copy-start | bytes 393220
  125.3 3.5 copy-start.3
  128.7 6.6 copy-start.1
  140.7 3.9 copy-start.13
  144.7 9.0 %copy-start.17 = (bf16[256,128]{1,0:T(8,128)(2,1)S(1)}, bf16[256,128]{1,0:T(8,128)(2,1)}, u32[]{:S(2)}) copy-start(bf16[256,128]{1,0:T(8,128)(2,1)} %param.32) | copy-start | bytes 196612
  144.7 9.0 %copy-start.21 = (f32[128,256]{1,0:T(8,128)S(1)}, f32[128,256]{1,0:T(8,128)}, u32[]{:S(2)}) copy-start(f32[128,256]{1,0:T(8,128)} %copy-done.20) | copy-start | bytes 393220
  146.6 31.0 %all-to-all-start.1 = ((bf16[128,32,128]{2,0,1:T(8,128)(2,1)}), bf16[128,32,128]{2,0,1:T(8,128)(2,1)S(1)}, u32[]{:S(2)}, u32[]{:S(2)}) async-start(bf16[128,32,128]{2,0,1:T(8,128)(2,1)} %copy.53), calls=%async_computation.1 | async-start | bytes 2097152 | tf_op jit(solution)/shard_map/all_to_all | solution.py:177
  152.9 279.6 %all-reduce.4.cloned.1.call-start = ((), (), s32[]{:S(2)}) async-start(), calls=%async_computation.6 | async-start | bytes 1310720 | tf_op jit(solution)/shard_map/psum | solution.py:193
  154.4 23.5 %copy-start.22 = (bf16[128,256]{1,0:T(8,128)(2,1)}, bf16[128,256]{1,0:T(8,128)(2,1)S(1)}, u32[]{:S(2)}) copy-start(bf16[128,256]{1,0:T(8,128)(2,1)S(1)} %get-tuple-element.280) | copy-start | bytes 196612
  156.4 501.1 %reduce-scatter.2.cloned.1.call-start = ((), (), s32[]{:S(2)}) async-start(), calls=%async_computation.5 | async-start | bytes 2162688 | tf_op jit(solution)/shard_map/reduce_scatter | solution.py:191
  177.9 30.7 %copy-start.5 = (f32[2048,128]{1,0:T(8,128)S(1)}, f32[2048,128]{1,0:T(8,128)}, u32[]{:S(2)}) copy-start(f32[2048,128]{1,0:T(8,128)} %custom-call.1) | copy-start | bytes 3145732
  236.5 2.9 copy-start.2
  236.5 2.9 copy-start.4
  236.5 3.2 copy-start.7
  236.5 3.2 copy-start.23
  239.4 0.7 copy-start.10
  239.4 0.8 copy-start.14
  239.4 0.8 copy-start.15
Sparse Core Ops, SparseCore 0:
  10.1 48.4 all-gather.2
  60.7 47.3 all-gather.4
  159.3 273.1 all-reduce.3
  437.9 219.5 reduce-scatter.1
where the time goes:
time: 674 us; the launch traced here: 668 us
  waiting for transfers between devices  360 us (53%)
  matrix products  141 us (21%)
  blocking collectives  105 us (16%)
  local copies, waits for them, and re-layouts  25.8 us (4%)
  starting transfers between devices  16.3 us (2%)
  between operations  14.7 us (2%)
    reduce_scatter x1, waiting for transfers between devices, local(): lax.psum_scatter(local_grad, 'dp', scatter_dimension=1, tiled=True)  225 us
    psum x1, blocking collectives, local(): lax.psum((partial_grads[0], partial_grads[1], partial_grads[2], partial_g...  105 us
    psum x1, waiting for transfers between devices, local(): lax.psum((partial_grads[0], partial_grads[1], partial_grads[2], partial_g...  87.7 us
    dot_general x4, matrix products, pool_one_block(): return jnp.dot(hit_table, table_rows, preferred_element_type=jnp.float32)  66.9 us
    dot_general x4, matrix products, shard_one_block(): lax.dot_general(hit_table, inputs[2], (((0,), (0,)), ((), ())), preferred...  57.6 us
    all_to_all x1, waiting for transfers between devices, local(): lax.all_to_all(pooled, 'table', split_axis=0, concat_axis=1, tiled=True)  24.2 us
    all_to_all x1, waiting for transfers between devices, local(): lax.all_to_all(shard_grads, 'table', split_axis=1, concat_axis=0, tiled=T...  21.2 us
  transfers between devices with their start and end apart: 6, of which 4 were waited for; matrix products, arithmetic and copies ran while one was open for 23% of the time, Pallas kernels for 0%

commit v1 on v0

--- a/solution.py
+++ b/solution.py
@@ -191,16 +191,19 @@
     table_grad = lax.psum_scatter(local_grad, "dp", scatter_dimension=1, tiled=True)
     partial_grads = bottom_back(dense_feats, saved, second_layer, third_layer, bottom_grad)
     summed = lax.psum(
-        (
-            partial_grads[0],
-            partial_grads[1],
-            partial_grads[2],
-            partial_grads[3],
-            partial_grads[4],
-            partial_grads[5],
-            bias_part,
+        lax.psum(
+            (
+                partial_grads[0],
+                partial_grads[1],
+                partial_grads[2],
+                partial_grads[3],
+                partial_grads[4],
+                partial_grads[5],
+                bias_part,
+            ),
+            "table",
         ),
-        ("dp", "table"),
+        "dp",
     )
     return (table_grad, summed[0], summed[1], summed[2], summed[3], summed[4], summed[5], summed[6])
 

time: 674 us -> 683 us (1.013)
  blocking collectives: 105 us -> 191 us
  waiting for transfers between devices: 360 us -> 282 us
    psum x0 -> x1, blocking collectives: none -> 144 us  [local(): lax.psum(lax.psum((partial_grads[0], partial_grads[1], partial_grads[2],...]
    reduce_scatter x1, waiting for transfers between devices: 225 us -> 136 us  [local(): lax.psum_scatter(local_grad, 'dp', scatter_dimension=1, tiled=True)]
    psum x1, blocking collectives: 105 us -> 47.9 us  [local(): lax.psum((partial_grads[0], partial_grads[1], partial_grads[2], partial_g...]
    psum x1, waiting for transfers between devices: 87.7 us -> 120 us  [local(): lax.psum((partial_grads[0], partial_grads[1], partial_grads[2], partial_g...]
    all_to_all x1, waiting for transfers between devices: 21.2 us -> 0.01 us  [local(): lax.all_to_all(shard_grads, 'table', split_axis=1, concat_axis=0, tiled=T...]
  transfers between devices with their start and end apart: 6 -> 7, of which waited for: 4 -> 3; matrix products, arithmetic and copies ran while one was open for 23% -> 22% of each run, Pallas kernels for 0% -> 0%
where the time goes in v1:
time: 683 us; the launch traced here: 677 us
  waiting for transfers between devices  282 us (41%)
  blocking collectives  191 us (28%)
  matrix products  141 us (21%)
  local copies, waits for them, and re-layouts  25.8 us (4%)
  starting transfers between devices  16.3 us (2%)
  between operations  14.7 us (2%)
    psum x1, blocking collectives, local(): lax.psum(lax.psum((partial_grads[0], partial_grads[1], partial_grads[2],...  144 us
    reduce_scatter x1, waiting for transfers between devices, local(): lax.psum_scatter(local_grad, 'dp', scatter_dimension=1, tiled=True)  136 us
    psum x1, waiting for transfers between devices, local(): lax.psum((partial_grads[0], partial_grads[1], partial_grads[2], partial_g...  120 us
    dot_general x4, matrix products, pool_one_block(): return jnp.dot(hit_table, table_rows, preferred_element_type=jnp.float32)  66.9 us
    dot_general x4, matrix products, shard_one_block(): lax.dot_general(hit_table, inputs[2], (((0,), (0,)), ((), ())), preferred...  57.5 us
    psum x1, blocking collectives, local(): lax.psum((partial_grads[0], partial_grads[1], partial_grads[2], partial_g...  47.9 us
    all_to_all x1, waiting for transfers between devices, local(): lax.all_to_all(pooled, 'table', split_axis=0, concat_axis=1, tiled=True)  24.2 us
  transfers between devices with their start and end apart: 7, of which 3 were waited for; matrix products, arithmetic and copies ran while one was open for 22% of the time, Pallas kernels for 0%

profile of v1, /device:TPU:8, one launch (start us, length us, event | category | flops | bytes accessed | tf_op | source)
XLA Modules:
  0.0 676.8 jit_solution(6967788535254718402)
XLA Ops:
  10.4 1.3 slice_bitcast_fusion.1
  11.8 33.8 %while.42 = (s32[]{:T(128)}, bf16[2,1024,128]{2,1,0:T(8,128)(2,1)S(1)}, s32[2,8,1024]{2,1,0:T(8,128)S(1)}, s32[2,1024]{1,0:T(2,128)S(1)}, bf16[2048,128]{1,0:T(8...) while((s32[]{:T(128)}, ...), condition=%wide.region_1.2_spmd, body=%wide.region_0.1_spmd.sunk | while | flops 620765184 | bytes 1167617 | solution.py:41
  11.9 16.7 %fusion.244 = bf16[2,1024,128]{2,1,0:T(8,128)(2,1)S(1)} fusion(bf16[2,1024,128]{2,1,0:T(8,128)(2,1)S(1)} %get-tuple-element.597, s32[]{:T(128)} %get-tuple-element.596, bf16[2048,128]{1,0:T(8,128)(2,1)S(1)} %get-tuple-element.614, s32[1024]{0:T(1024)S(1)} %bitcast.227, s32[1024]{0:T(1024)S(1)} %bitcast.221, s32[1024]{0:T(1024)S(1)} %bitcast.222, ...), kind=kOutput, calls=%fused_computation.41.clone.1 | convolution fusion | flops 620756992 | bytes 1089540 | tf_op jit(solution)/shard_map/while/body/eval_jaxpr/dot_general | solution.py:39
  28.8 16.7 %fusion.244 = bf16[2,1024,128]{2,1,0:T(8,128)(2,1)S(1)} fusion(bf16[2,1024,128]{2,1,0:T(8,128)(2,1)S(1)} %get-tuple-element.597, s32[]{:T(128)} %get-tuple-element.596, bf16[2048,128]{1,0:T(8,128)(2,1)S(1)} %get-tuple-element.614, s32[1024]{0:T(1024)S(1)} %bitcast.227, s32[1024]{0:T(1024)S(1)} %bitcast.221, s32[1024]{0:T(1024)S(1)} %bitcast.222, ...), kind=kOutput, calls=%fused_computation.41.clone.1 | convolution fusion | flops 620756992 | bytes 1089540 | tf_op jit(solution)/shard_map/while/body/eval_jaxpr/dot_general | solution.py:39
  45.7 33.8 %while.43 = (s32[]{:T(128)}, bf16[2,1024,128]{2,1,0:T(8,128)(2,1)S(1)}, s32[2,8,1024]{2,1,0:T(8,128)S(1)}, s32[2,1024]{1,0:T(2,128)S(1)}, bf16[2048,128]{1,0:T(8...) while((s32[]{:T(128)}, ...), condition=%wide.region_3.4_spmd, body=%wide.region_2.3_spmd.sunk | while | flops 620765184 | bytes 1167617 | solution.py:41
  45.8 16.7 %fusion.247 = bf16[2,1024,128]{2,1,0:T(8,128)(2,1)S(1)} fusion(bf16[2,1024,128]{2,1,0:T(8,128)(2,1)S(1)} %get-tuple-element.555, s32[]{:T(128)} %get-tuple-element.554, bf16[2048,128]{1,0:T(8,128)(2,1)S(1)} %get-tuple-element.572, s32[1024]{0:T(1024)S(1)} %bitcast.235, s32[1024]{0:T(1024)S(1)} %bitcast.229, s32[1024]{0:T(1024)S(1)} %bitcast.230, ...), kind=kOutput, calls=%fused_computation.100.clone.1 | convolution fusion | flops 620756992 | bytes 1089540 | tf_op jit(solution)/shard_map/while/body/eval_jaxpr/dot_general | solution.py:39
  62.7 16.7 %fusion.247 = bf16[2,1024,128]{2,1,0:T(8,128)(2,1)S(1)} fusion(bf16[2,1024,128]{2,1,0:T(8,128)(2,1)S(1)} %get-tuple-element.555, s32[]{:T(128)} %get-tuple-element.554, bf16[2048,128]{1,0:T(8,128)(2,1)S(1)} %get-tuple-element.572, s32[1024]{0:T(1024)S(1)} %bitcast.235, s32[1024]{0:T(1024)S(1)} %bitcast.229, s32[1024]{0:T(1024)S(1)} %bitcast.230, ...), kind=kOutput, calls=%fused_computation.100.clone.1 | convolution fusion | flops 620756992 | bytes 1089540 | tf_op jit(solution)/shard_map/while/body/eval_jaxpr/dot_general | solution.py:39
  79.6 9.5 %copy.44 = bf16[2048,2,128]{2,1,0:T(2,128)(2,1)} copy(bf16[2048,2,128]{2,0,1:T(8,128)(2,1)S(1)} %pad_maximum_fusion.1) | data formatting | bytes 2097152 | tf_op jit(solution)/shard_map/stack | solution.py:128
  89.1 9.8 %all-to-all-start = ((bf16[2048,2,128]{2,1,0:T(2,128)(2,1)}), bf16[2048,2,128]{2,1,0:T(2,128)(2,1)S(1)}, u32[]{:S(2)}, u32[]{:S(2)}) async-start(bf16[2048,2,128]{2,1,0:T(2,128)(2,1)} %copy.44), calls=%async_computation | async-start | bytes 2097152 | tf_op jit(solution)/shard_map/all_to_all | solution.py:137
  99.9 24.2 %all-to-all-done = bf16[2048,2,128]{2,1,0:T(2,128)(2,1)S(1)} async-done(((bf16[2048,2,128]{2,1,0:T(2,128)(2,1)}), bf16[2048,2,128]{2,1,0:T(2,128)(2,1)S(1)}, u32[]{:S(2)}, u32[]{:S(2)}) %all-to-all-start) | async-done | bytes 1048608 | tf_op jit(solution)/shard_map/all_to_all | solution.py:137
  124.2 1.1 copy.46
  126.4 1.3 copy.49
  127.7 1.0 copy.50
  128.8 6.5 fusion.187
  135.3 5.4 fusion.188
  142.7 1.9 copy.52
  145.2 1.4 copy.53
  146.6 6.3 all-to-all-start.1
  155.2 1.1 fusion.205
  156.4 120.2 %all-reduce.9.cloned.1.call-done = (f32[512,256]{1,0:T(8,128)}, f32[256,128]{1,0:T(8,128)}) async-done(((f32[512,256]{1,0:T(8,128)}, f32[256,128]{1,0:T(8,128)}), (f32[512,256]{1,0:T(8,128)}, f32[256,128]{1,0:T(8,128)})) %all-reduce.9.cloned.1.call-update) | async-done | bytes 655376 | tf_op jit(solution)/shard_map/psum | solution.py:194
  276.9 30.7 %while.44 = (s32[]{:T(128)}, f32[2048,128]{1,0:T(8,128)}, s32[2,8,1024]{2,1,0:T(8,128)S(1)}, s32[2,1024]{1,0:T(2,128)S(1)}, bf16[2,1024,128]{2,1,0:T(8,128)(2,1)...) while((s32[]{:T(128)}, f32[2048,128]{1,0:T(8,128)}, ...), condition=%wide.region_5.6_spmd.clone, body=%wide.region_4.5_spmd.clone.sunk | while | flops 621289472 | bytes 2478347 | solution.py:56
  277.3 14.5 %fusion.250 = f32[2048,128]{1,0:T(8,128)} fusion(s32[1024]{0:T(1024)S(1)} %bitcast.211, s32[1024]{0:T(1024)S(1)} %bitcast.205, s32[1024]{0:T(1024)S(1)} %bitcast.206, s32[1024]{0:T(1024)S(1)} %bitcast.207, s32[1024]{0:T(1024)S(1)} %bitcast.208, s32[1024]{0:T(1024)S(1)} %bitcast.209, s32[1024]{0:T(1024)S(1)} %bitcast.210, s32[1024]{0:T(1024)S(1)} %bitcast.204, ...), kind=kOutput, calls=%fused_computation.166.clone.1 | convolution fusion | flops 621281280 | bytes 2400261 | tf_op jit(solution)/shard_map/while/body/eval_jaxpr/dot_general | solution.py:51
  291.9 15.7 %fusion.250 = f32[2048,128]{1,0:T(8,128)} fusion(s32[1024]{0:T(1024)S(1)} %bitcast.211, s32[1024]{0:T(1024)S(1)} %bitcast.205, s32[1024]{0:T(1024)S(1)} %bitcast.206, s32[1024]{0:T(1024)S(1)} %bitcast.207, s32[1024]{0:T(1024)S(1)} %bitcast.208, s32[1024]{0:T(1024)S(1)} %bitcast.209, s32[1024]{0:T(1024)S(1)} %bitcast.210, s32[1024]{0:T(1024)S(1)} %bitcast.204, ...), kind=kOutput, calls=%fused_computation.166.clone.1 | convolution fusion | flops 621281280 | bytes 2400261 | tf_op jit(solution)/shard_map/while/body/eval_jaxpr/dot_general | solution.py:51
  307.6 27.9 %while.45 = (s32[]{:T(128)}, f32[2048,128]{1,0:T(8,128)S(1)}, s32[2,8,1024]{2,1,0:T(8,128)S(1)}, s32[2,1024]{1,0:T(2,128)S(1)}, bf16[2,1024,128]{2,1,0:T(8,128)(...) while((s32[]{:T(128)}, f32[2048,128]{1,0:T(8,128)S(1)}, ...), condition=%wide.region_7.8_spmd.clone, body=%wide.region_6.7_spmd.clone.sunk | while | flops 621289472 | bytes 2478347 | solution.py:56
  308.0 13.7 %fusion.253 = f32[2048,128]{1,0:T(8,128)S(1)} fusion(s32[1024]{0:T(1024)S(1)} %bitcast.219, s32[1024]{0:T(1024)S(1)} %bitcast.213, s32[1024]{0:T(1024)S(1)} %bitcast.214, s32[1024]{0:T(1024)S(1)} %bitcast.215, s32[1024]{0:T(1024)S(1)} %bitcast.216, s32[1024]{0:T(1024)S(1)} %bitcast.217, s32[1024]{0:T(1024)S(1)} %bitcast.218, ...), kind=kOutput, calls=%fused_computation.235.clone.1 | convolution fusion | flops 621281280 | bytes 2400261 | tf_op jit(solution)/shard_map/while/body/eval_jaxpr/dot_general | solution.py:51
  321.9 13.7 %fusion.253 = f32[2048,128]{1,0:T(8,128)S(1)} fusion(s32[1024]{0:T(1024)S(1)} %bitcast.219, s32[1024]{0:T(1024)S(1)} %bitcast.213, s32[1024]{0:T(1024)S(1)} %bitcast.214, s32[1024]{0:T(1024)S(1)} %bitcast.215, s32[1024]{0:T(1024)S(1)} %bitcast.216, s32[1024]{0:T(1024)S(1)} %bitcast.217, s32[1024]{0:T(1024)S(1)} %bitcast.218, ...), kind=kOutput, calls=%fused_computation.235.clone.1 | convolution fusion | flops 621281280 | bytes 2400261 | tf_op jit(solution)/shard_map/while/body/eval_jaxpr/dot_general | solution.py:51
  335.6 2.9 pad_maximum_fusion
  339.3 47.9 %all-reduce.2 = (f32[13,512]{1,0:T(8,128)S(1)}, f32[512]{0:T(512)S(1)}, f32[256]{0:T(256)S(1)}, f32[128]{0:T(128)S(1)}, f32[3456]{0:T(1024)S(1)}) all-reduce(f32[13,512]{1,0:T(8,128)S(1)} %convolution_bitcast_fusion, f32[512]{0:T(512)S(1)} %get-tuple-element.284, ...), channel_id=1, replica_groups=mesh['dp'=32,'table'=16] {'table'}, use_global_device_ids=true, to_apply=%region_9.10 | all-reduce | flops 11008 | bytes 88064 | tf_op jit(solution)/shard_map/psum | solution.py:194
  387.1 143.6 %all-reduce = (f32[13,512]{1,0:T(8,128)}, f32[512]{0:T(512)}, f32[256]{0:T(256)}, f32[128]{0:T(128)}, f32[3456]{0:T(1024)}) all-reduce(f32[13,512]{1,0:T(8,128)S(1)} %get-tuple-element.237, f32[512]{0:T(512)S(1)} %get-tuple-element.238, f32[256]{0:T(256)S(1)} %get-tuple-element.239, ...), channel_id=1, replica_groups=mesh['dp'=32,'table'=16] {'dp'}, use_global_device_ids=true, to_apply=%region_10.11 | all-reduce | flops 11008 | bytes 88064 | tf_op jit(solution)/shard_map/psum | solution.py:193
  530.7 135.7 %reduce-scatter.2.cloned.1.call-done = f32[2,64,128]{2,1,0:T(8,128)} async-done(((f32[2,2048,128]{2,1,0:T(8,128)}), f32[2,64,128]{2,1,0:T(8,128)}) %reduce-scatter.2.cloned.1.call-update) | async-done | bytes 65552 | tf_op jit(solution)/shard_map/reduce_scatter | solution.py:191
  666.4 1.9 copy.87
  668.3 1.6 copy.88
  (104 shorter events, 12.6 us)
Async XLA Ops:
  7.2 92.0 %copy-start = (bf16[512,256]{1,0:T(8,128)(2,1)S(1)}, bf16[512,256]{1,0:T(8,128)(2,1)}, u32[]{:S(2)}) copy-start(bf16[512,256]{1,0:T(8,128)(2,1)} %param.30) | copy-start | bytes 786436
  7.2 121.6 %all-gather.3.cloned.1.call-start = ((), (), s32[]{:S(2)}) async-start(), calls=%async_computation.3 | async-start | bytes 3760128 | tf_op jit(solution)/shard_map/all_gather | solution.py:156
  7.9 120.9 %all-gather.5.cloned.1.call-start = ((), (), s32[]{:S(2)}) async-start(), calls=%async_computation.4 | async-start | bytes 3760128 | tf_op jit(solution)/shard_map/all_gather | solution.py:157
  79.5 19.5 %copy-start.7 = (bf16[13,512]{1,0:T(8,128)(2,1)S(1)}, bf16[13,512]{1,0:T(8,128)(2,1)}, u32[]{:S(2)}) copy-start(bf16[13,512]{1,0:T(8,128)(2,1)} %param.28) | copy-start | bytes 39940
  79.5 19.5 %copy-start.8 = (bf16[128,13]{0,1:T(8,128)(2,1)S(1)}, bf16[128,13]{0,1:T(8,128)(2,1)}, u32[]{:S(2)}) copy-start(bf16[128,13]{0,1:T(8,128)(2,1)} %param.23) | copy-start | bytes 9988
  79.5 19.5 %copy-start.10 = (f32[512]{0:T(512)S(1)}, f32[512]{0:T(512)}, u32[]{:S(2)}) copy-start(f32[512]{0:T(512)} %param.29) | copy-start | bytes 6148
  79.5 19.7 %copy-start.17 = (f32[256]{0:T(256)S(1)}, f32[256]{0:T(256)}, u32[]{:S(2)}) copy-start(f32[256]{0:T(256)} %param.31) | copy-start | bytes 3076
  79.5 19.9 %copy-start.15 = (bf16[256,128]{1,0:T(8,128)(2,1)S(1)}, bf16[256,128]{1,0:T(8,128)(2,1)}, u32[]{:S(2)}) copy-start(bf16[256,128]{1,0:T(8,128)(2,1)} %param.32) | copy-start | bytes 196612
  79.5 19.9 %copy-start.18 = (f32[128]{0:T(128)S(1)}, f32[128]{0:T(128)}, u32[]{:S(2)}) copy-start(f32[128]{0:T(128)} %param.33) | copy-start | bytes 1540
  89.1 34.9 %all-to-all-start = ((bf16[2048,2,128]{2,1,0:T(2,128)(2,1)}), bf16[2048,2,128]{2,1,0:T(2,128)(2,1)S(1)}, u32[]{:S(2)}, u32[]{:S(2)}) async-start(bf16[2048,2,128]{2,1,0:T(2,128)(2,1)} %copy.44), calls=%async_computation | async-start | bytes 2097152 | tf_op jit(solution)/shard_map/all_to_all | solution.py:137
  99.0 26.3 %copy-start.11 = (s32[32]{0:T(128)S(1)}, s32[32]{0:T(128)}, u32[]{:S(2)}) copy-start(s32[32]{0:T(128)} %param.26) | copy-start | bytes 388
  99.2 56.0 %copy-start.5 = (f32[128,512]{1,0:T(8,128)}, f32[128,512]{1,0:T(8,128)S(1)}, u32[]{:S(2)}) copy-start(f32[128,512]{1,0:T(8,128)S(1)} %convolution_add_fusion.2) | copy-start | bytes 786436
  99.5 26.4 %copy-start.19 = (f32[128,256]{1,0:T(8,128)}, f32[128,256]{1,0:T(8,128)S(1)}, u32[]{:S(2)}) copy-start(f32[128,256]{1,0:T(8,128)S(1)} %convolution_add_fusion.3) | copy-start | bytes 393220
  125.3 3.5 copy-start.3
  128.7 6.6 copy-start.1
  140.7 3.9 copy-start.12
  144.7 8.9 %copy-start.16 = (bf16[256,128]{1,0:T(8,128)(2,1)S(1)}, bf16[256,128]{1,0:T(8,128)(2,1)}, u32[]{:S(2)}) copy-start(bf16[256,128]{1,0:T(8,128)(2,1)} %param.32) | copy-start | bytes 196612
  144.7 8.9 %copy-start.20 = (f32[128,256]{1,0:T(8,128)S(1)}, f32[128,256]{1,0:T(8,128)}, u32[]{:S(2)}) copy-start(f32[128,256]{1,0:T(8,128)} %copy-done.19) | copy-start | bytes 393220
  146.6 130.2 %all-to-all-start.1 = ((bf16[128,32,128]{2,0,1:T(8,128)(2,1)}), bf16[128,32,128]{2,0,1:T(8,128)(2,1)S(1)}, u32[]{:S(2)}, u32[]{:S(2)}) async-start(bf16[128,32,128]{2,0,1:T(8,128)(2,1)} %copy.53), calls=%async_computation.1 | async-start | bytes 2097152 | tf_op jit(solution)/shard_map/all_to_all | solution.py:177
  152.9 123.8 %all-reduce.9.cloned.1.call-start = ((), (), s32[]{:S(2)}) async-start(), calls=%async_computation.7 | async-start | bytes 1310720 | tf_op jit(solution)/shard_map/psum | solution.py:194
  154.3 2.1 copy-start.21
  156.3 374.4 %all-reduce.7.cloned.1.call-start = ((), (), s32[]{:S(2)}) async-start(), calls=%async_computation.6 | async-start | bytes 1310720 | tf_op jit(solution)/shard_map/psum | solution.py:193
  276.7 389.8 %reduce-scatter.2.cloned.1.call-start = ((), (), s32[]{:S(2)}) async-start(), calls=%async_computation.5 | async-start | bytes 2162688 | tf_op jit(solution)/shard_map/reduce_scatter | solution.py:191
  335.5 2.9 copy-start.2
  335.6 2.9 copy-start.4
  335.6 3.2 copy-start.6
  335.6 3.2 copy-start.22
  338.4 0.7 copy-start.9
  338.4 0.8 copy-start.13
  338.4 0.8 copy-start.14
Sparse Core Ops, SparseCore 0:
  10.1 48.4 all-gather.2
  60.7 47.3 all-gather.4
  156.7 119.8 all-reduce.8
  280.3 162.2 all-reduce.6
  447.4 218.9 reduce-scatter.1
